TPU v7x, 32 devices: a whole 2x2x4 slice. The times are simulated.
32 devices in a mesh: member: 2 (over y), lon: 4 (over x, core), lat: 4 (over z).
Axes of the slice: x: 2, y: 2, z: 4, core: 2. Of those that a mesh axis runs over, the one named last changes fastest.
Arguments:
- heat_content: float32 [32, 256, 512], P(None, ('member', 'lat'), 'lon'), parts along dimension 1, may hold values from -6 to 6
- sea_height: float32 [256, 512], P(('member', 'lat'), 'lon'), parts along dimension 0, may hold values from -6 to 6
- closing_heat_sensitivity: float32 [32, 256, 512], P(None, ('member', 'lat'), 'lon'), parts along dimension 1, may hold values from -6 to 6
- closing_height_sensitivity: float32 [256, 512], P(('member', 'lat'), 'lon'), parts along dimension 0, may hold values from -6 to 6
- mixing_coefficient: float32 [128, 512], P('lat', 'lon'), may hold values from 0.02 to 0.2
- sea_indicator: int32 [128, 512], P('lat', 'lon'), may hold values 0 or 1
- water_layer_count: int32 [128, 512], P('lat', 'lon'), may hold values from 1 to 32
Outputs:
- temperature_grad: float32 [32, 256, 512], P(None, ('member', 'lat'), 'lon'), parts along dimension 1
- surface_grad: float32 [256, 512], P(('member', 'lat'), 'lon'), parts along dimension 0
- diffusivity_grad: float32 [256, 512], P(('member', 'lat'), 'lon'), parts along dimension 0
There are 2 independent parts, one for each index of `member`. A program takes and returns all parts, laid end to end along the dimension named above; an argument that names none is the same for every part. Nothing has to cross between parts.
All inputs are finite; a program needn't handle non-finite values. No bound on the sum of `sea_indicator` on one device may be relied on, other than what follows from the above.
Results may differ from a plain program's by a relative error of at most 0.0001.
Values sent between devices are 32-bit elements; how exact they have to be, the bound alone decides.
A program may use at most 64 MiB of HBM per device.

v0:
```python
import math

import jax
import jax.numpy as jnp
from jax import lax
from jax.sharding import PartitionSpec as P

ITERS = 4


EOS_QUAD = 0.1
PRESS_COEF = 0.5
SURF_COEF = 4.0
COUPLING = 1.0


def extended(x, sides, width):
    for axis, dim in sides:
        devices, length = (lax.axis_size(axis), x.shape[dim])
        up = [(i, (i + 1) % devices) for i in range(devices)]
        down = [(j, i) for i, j in up]
        last = lax.slice_in_dim(x, length - width, length, axis=dim)
        initial = lax.slice_in_dim(x, 0, width, axis=dim)
        before = lax.ppermute(last, axis, up)
        after = lax.ppermute(initial, axis, down)
        x = jnp.concatenate([before, x, after], axis=dim)
    return x


def laplace_padded(padded, weight_x, weight_y):
    centre = padded[..., 1:-1, 1:-1]
    eastern = weight_x[..., 1:] * (padded[..., 1:-1, 2:] - centre)
    western = weight_x[..., :-1] * (centre - padded[..., 1:-1, :-2])
    northern = weight_y[..., 1:, :] * (padded[..., 2:, 1:-1] - centre)
    southern = weight_y[..., :-1, :] * (centre - padded[..., :-2, 1:-1])
    return eastern - western + northern - southern


def three_dim_rim(field):
    return extended(field, (("lon", 2), ("lat", 1)), 1)


def horizontal_rim_halo(field):
    return extended(field, (("lon", 1), ("lat", 0)), 1)


def evaluate_hydrostatic_load(state, water_site_indicator):
    running_count = state.shape[0]
    heights = (jnp.arange(running_count, dtype=jnp.float32)[:, None, None] + 0.5) / running_count
    return jnp.sum(
        water_site_indicator * heights * (state + EOS_QUAD * state * state), axis=0
    ) / math.sqrt(running_count)


def apply_surface(direction, eastward_thickness, northward_thickness):
    padded = extended(direction, (("lon", 2), ("lat", 1)), 1)
    return direction - SURF_COEF * laplace_padded(padded, eastward_thickness, northward_thickness)


def member_sum(field):
    return jnp.sum(field, axis=(1, 2))


def squares(residual):
    return lax.psum(member_sum(residual * residual), ("lon", "lat"))


def spread(scalars):
    return scalars[:, None, None]


def poisson_inversion(rhs, eastward_thickness, northward_thickness):
    solution = jnp.zeros_like(rhs)
    residual = rhs
    direction = rhs
    norm_now = squares(residual)
    for iteration in range(ITERS):
        image = apply_surface(direction, eastward_thickness, northward_thickness)
        curve = lax.psum(member_sum(direction * image), ("lon", "lat"))
        step_size = norm_now / curve
        solution = solution + spread(step_size) * direction
        residual = residual - spread(step_size) * image
        norm_next = squares(residual)
        direction = residual + spread(norm_next / norm_now) * direction
        norm_now = norm_next
    return solution


def shards(
    heat_content,
    sea_height,
    closing_heat_sensitivity,
    closing_height_sensitivity,
    mixing_coefficient,
    sea_indicator,
    water_layer_count,
):
    running_count, parallel_lines, meridian_lines = heat_content.shape
    depth_levels = jnp.arange(running_count, dtype=jnp.float32)[:, None, None]
    land_f = sea_indicator.astype(jnp.float32)
    bottom_f = water_layer_count.astype(jnp.float32)
    water_site_indicator = land_f[None] * (depth_levels < bottom_f[None]).astype(jnp.float32)
    depth_col = jnp.sum(water_site_indicator, axis=0) / running_count
    static = jnp.stack([land_f, bottom_f, mixing_coefficient, depth_col])
    primed_sensitivity = water_site_indicator * closing_heat_sensitivity
    static_p = extended(static, (("lon", 2), ("lat", 1)), 1)
    front_piece = three_dim_rim(heat_content)
    lat_index = lax.axis_index("lat")
    lat_count = lax.axis_size("lat")
    row_ids = jnp.arange(parallel_lines + 2)
    closed = jnp.logical_or(
        jnp.logical_and(row_ids == 0, lat_index == 0),
        jnp.logical_and(row_ids == parallel_lines + 1, lat_index == lat_count - 1),
    )
    keep_rows = 1.0 - closed.astype(jnp.float32)
    land_p = static_p[0] * keep_rows[:, None]
    wet_p = land_p[None] * (depth_levels < static_p[1][None]).astype(jnp.float32)
    kappa_p = static_p[2]
    depth_p = static_p[3]
    wet_x = wet_p[:, 1:-1, :-1] * wet_p[:, 1:-1, 1:]
    wet_y = wet_p[:, :-1, 1:-1] * wet_p[:, 1:, 1:-1]
    kappa_x = 0.5 * (kappa_p[1:-1, :-1] + kappa_p[1:-1, 1:]) * wet_x
    kappa_y = 0.5 * (kappa_p[:-1, 1:-1] + kappa_p[1:, 1:-1]) * wet_y
    land_x = land_p[1:-1, :-1] * land_p[1:-1, 1:]
    land_y = land_p[:-1, 1:-1] * land_p[1:, 1:-1]
    eastward_thickness = jnp.minimum(depth_p[1:-1, :-1], depth_p[1:-1, 1:]) * land_x
    northward_thickness = jnp.minimum(depth_p[:-1, 1:-1], depth_p[1:, 1:-1]) * land_y
    profile = 1.0 - depth_levels / running_count
    heights = (depth_levels + 0.5) / running_count
    hydrostatic_share = horizontal_rim_halo(
        evaluate_hydrostatic_load(heat_content, water_site_indicator)
    )
    rhs = sea_height - PRESS_COEF * laplace_padded(hydrostatic_share, land_x, land_y)
    total_one = closing_height_sensitivity + COUPLING * jnp.sum(
        profile * primed_sensitivity, axis=0
    )
    surface_next = poisson_inversion(rhs[None], eastward_thickness, northward_thickness)[0]
    back_one = poisson_inversion(total_one[None], eastward_thickness, northward_thickness)[0]
    trailing_piece = water_site_indicator * (
        heat_content
        + laplace_padded(front_piece, kappa_x, kappa_y)
        + COUPLING * profile * surface_next[None]
    )
    second_p, seeded_p = (
        extended(trailing_piece, (("lon", 2), ("lat", 1)), 1),
        extended(primed_sensitivity, (("lon", 2), ("lat", 1)), 1),
    )

    def reverse_sweep_once(state, state_p, masked, masked_p, back_rhs):
        back_temp = masked + laplace_padded(masked_p, kappa_x, kappa_y)
        grad_x = jnp.sum(
            wet_x
            * (state_p[:, 1:-1, 1:] - state_p[:, 1:-1, :-1])
            * (masked_p[:, 1:-1, :-1] - masked_p[:, 1:-1, 1:]),
            axis=0,
        )
        grad_y = jnp.sum(
            wet_y
            * (state_p[:, 1:, 1:-1] - state_p[:, :-1, 1:-1])
            * (masked_p[:, :-1, 1:-1] - masked_p[:, 1:, 1:-1]),
            axis=0,
        )
        grad_kappa = 0.5 * (grad_x[:, 1:] + grad_x[:, :-1] + grad_y[1:, :] + grad_y[:-1, :])
        back_press = -PRESS_COEF * laplace_padded(horizontal_rim_halo(back_rhs), land_x, land_y)
        back_temp = back_temp + water_site_indicator * heights * (
            1.0 + 2.0 * EOS_QUAD * state
        ) * back_press[None] / math.sqrt(running_count)
        return (back_temp, back_rhs, grad_kappa)

    heat_content_later, sea_height_later, sensitivity_later_moment = reverse_sweep_once(
        trailing_piece, second_p, primed_sensitivity, seeded_p, back_one
    )
    starting_land_zeroed = water_site_indicator * heat_content_later
    total_zero = sea_height_later + COUPLING * jnp.sum(profile * starting_land_zeroed, axis=0)
    opening_reverse_sweep = poisson_inversion(
        total_zero[None], eastward_thickness, northward_thickness
    )[0]
    heat_content_earlier, sea_height_earlier, sensitivity_earlier_moment = reverse_sweep_once(
        heat_content,
        front_piece,
        starting_land_zeroed,
        three_dim_rim(starting_land_zeroed),
        opening_reverse_sweep,
    )
    return (
        heat_content_earlier,
        sea_height_earlier,
        sensitivity_later_moment + sensitivity_earlier_moment,
    )


def solution(mesh):
    placed = (
        P(None, ("member", "lat"), "lon"),
        P(("member", "lat"), "lon"),
        P(None, ("member", "lat"), "lon"),
        P(("member", "lat"), "lon"),
        P("lat", "lon"),
        P("lat", "lon"),
        P("lat", "lon"),
    )
    return jax.shard_map(
        shards,
        mesh=mesh,
        in_specs=placed,
        out_specs=(
            P(None, ("member", "lat"), "lon"),
            P(("member", "lat"), "lon"),
            P(("member", "lat"), "lon"),
        ),
        check_vma=False,
    )
```

profile of v0, /device:TPU:0, one launch (start us, length us, event | category | flops | bytes accessed | tf_op | source)
XLA Modules:
  0.0 676.4 jit_solution(12926336848230053775)
XLA Ops:
  17.2 3.7 collective-permute-start.3
  22.4 3.8 collective-permute-done.2
  35.3 2.4 collective-permute-start.34
  39.2 3.8 collective-permute-start.18
  45.3 32.9 %all-reduce.7 = (f32[1]{0:T(128)}, f32[1]{0:T(128)}, f32[1]{0:T(128)}, f32[1]{0:T(128)}) all-reduce(f32[1]{0:T(128)} %bitcast.8, f32[1]{0:T(128)} %bitcast.15, f32[1]{0:T(128)} %bitcast.32, f32[1]{0:T(128)} %bitcast.34), channel_id=1, replica_groups=mesh['member'=2,'lon'=4,'lat'=4] {'lon','lat'}, use_global_device_ids=true, to_apply=%region_3.0 | all-reduce | flops 4 | bytes 32 | tf_op jit(solution)/shard_map/psum | solution.py:65
  82.1 30.4 %all-reduce.6 = (f32[1]{0:T(128)}, f32[1]{0:T(128)}) all-reduce(f32[1]{0:T(128)} %bitcast.18, f32[1]{0:T(128)} %bitcast.37), channel_id=1, replica_groups=mesh['member'=2,'lon'=4,'lat'=4] {'lon','lat'}, use_global_device_ids=true, to_apply=%region_7.0 | all-reduce | flops 2 | bytes 16 | tf_op jit(solution)/shard_map/psum | solution.py:65
  125.1 3.4 collective-permute-start.22
  131.4 33.1 %all-reduce.5 = (f32[1]{0:T(128)}, f32[1]{0:T(128)}) all-reduce(f32[1]{0:T(128)} %bitcast.21, f32[1]{0:T(128)} %bitcast.40), channel_id=1, replica_groups=mesh['member'=2,'lon'=4,'lat'=4] {'lon','lat'}, use_global_device_ids=true, to_apply=%region_9.0 | all-reduce | flops 2 | bytes 16 | tf_op jit(solution)/shard_map/psum | solution.py:79
  171.2 30.3 %all-reduce.4 = (f32[1]{0:T(128)}, f32[1]{0:T(128)}) all-reduce(f32[1]{0:T(128)} %bitcast.23, f32[1]{0:T(128)} %bitcast.42), channel_id=1, replica_groups=mesh['member'=2,'lon'=4,'lat'=4] {'lon','lat'}, use_global_device_ids=true, to_apply=%region_11.0 | all-reduce | flops 2 | bytes 16 | tf_op jit(solution)/shard_map/psum | solution.py:65
  218.0 3.4 collective-permute-start.42
  224.3 3.7 collective-permute-start.6
  229.5 31.7 %all-reduce.3 = (f32[1]{0:T(128)}, f32[1]{0:T(128)}) all-reduce(f32[1]{0:T(128)} %bitcast.25, f32[1]{0:T(128)} %bitcast.44), channel_id=1, replica_groups=mesh['member'=2,'lon'=4,'lat'=4] {'lon','lat'}, use_global_device_ids=true, to_apply=%region_13.0 | all-reduce | flops 2 | bytes 16 | tf_op jit(solution)/shard_map/psum | solution.py:79
  266.7 31.2 %all-reduce.2 = (f32[1]{0:T(128)}, f32[1]{0:T(128)}) all-reduce(f32[1]{0:T(128)} %bitcast.27, f32[1]{0:T(128)} %bitcast.46), channel_id=1, replica_groups=mesh['member'=2,'lon'=4,'lat'=4] {'lon','lat'}, use_global_device_ids=true, to_apply=%region_15.0 | all-reduce | flops 2 | bytes 16 | tf_op jit(solution)/shard_map/psum | solution.py:65
  310.8 3.8 collective-permute-start.46
  316.9 32.9 %all-reduce.1 = (f32[1]{0:T(128)}, f32[1]{0:T(128)}) all-reduce(f32[1]{0:T(128)} %bitcast.29, f32[1]{0:T(128)} %bitcast.48), channel_id=1, replica_groups=mesh['member'=2,'lon'=4,'lat'=4] {'lon','lat'}, use_global_device_ids=true, to_apply=%region_17.0 | all-reduce | flops 2 | bytes 16 | tf_op jit(solution)/shard_map/psum | solution.py:79
  355.2 3.8 collective-permute-start.50
  364.5 4.9 multiply_reduce_fusion
  373.1 3.6 collective-permute-start.58
  378.9 32.3 %all-reduce = (f32[1]{0:T(128)}, f32[1]{0:T(128)}) all-reduce(f32[1]{0:T(128)} %bitcast.52, f32[1]{0:T(128)} %bitcast.53), channel_id=1, replica_groups=mesh['member'=2,'lon'=4,'lat'=4] {'lon','lat'}, use_global_device_ids=true, to_apply=%region_37.0 | all-reduce | flops 2 | bytes 16 | tf_op jit(solution)/shard_map/psum | solution.py:65
  413.2 30.6 %psum.186 = f32[1]{0:T(128)} all-reduce(f32[1]{0:T(128)} %bitcast.55), channel_id=1, replica_groups=mesh['member'=2,'lon'=4,'lat'=4] {'lon','lat'}, use_global_device_ids=true, to_apply=%region_41.0 | all-reduce | flops 1 | bytes 8 | tf_op jit(solution)/shard_map/psum | solution.py:65
  454.7 32.1 %psum.187 = f32[1]{0:T(128)} all-reduce(f32[1]{0:T(128)} %bitcast.57), channel_id=1, replica_groups=mesh['member'=2,'lon'=4,'lat'=4] {'lon','lat'}, use_global_device_ids=true, to_apply=%region_43.0 | all-reduce | flops 1 | bytes 8 | tf_op jit(solution)/shard_map/psum | solution.py:79
  488.9 30.7 %psum.188 = f32[1]{0:T(128)} all-reduce(f32[1]{0:T(128)} %bitcast.59), channel_id=1, replica_groups=mesh['member'=2,'lon'=4,'lat'=4] {'lon','lat'}, use_global_device_ids=true, to_apply=%region_45.0 | all-reduce | flops 1 | bytes 8 | tf_op jit(solution)/shard_map/psum | solution.py:65
  530.5 32.2 %psum.189 = f32[1]{0:T(128)} all-reduce(f32[1]{0:T(128)} %bitcast.61), channel_id=1, replica_groups=mesh['member'=2,'lon'=4,'lat'=4] {'lon','lat'}, use_global_device_ids=true, to_apply=%region_47.0 | all-reduce | flops 1 | bytes 8 | tf_op jit(solution)/shard_map/psum | solution.py:79
  564.6 30.7 %psum.190 = f32[1]{0:T(128)} all-reduce(f32[1]{0:T(128)} %bitcast.63), channel_id=1, replica_groups=mesh['member'=2,'lon'=4,'lat'=4] {'lon','lat'}, use_global_device_ids=true, to_apply=%region_49.0 | all-reduce | flops 1 | bytes 8 | tf_op jit(solution)/shard_map/psum | solution.py:65
  606.1 32.1 %psum.191 = f32[1]{0:T(128)} all-reduce(f32[1]{0:T(128)} %bitcast.65), channel_id=1, replica_groups=mesh['member'=2,'lon'=4,'lat'=4] {'lon','lat'}, use_global_device_ids=true, to_apply=%region_51.0 | all-reduce | flops 1 | bytes 8 | tf_op jit(solution)/shard_map/psum | solution.py:79
  644.1 3.3 collective-permute-start.74
  651.9 3.4 collective-permute-start.54
  655.2 4.1 collective-permute-done.76
  661.9 3.3 collective-permute-start.78
  665.2 2.6 fusion.8
  667.9 2.4 fusion.15
  673.1 3.3 fusion.29
  (307 shorter events, 141.1 us)
Async XLA Ops:
  5.1 8.4 %collective-permute-start.12 = (f32[32,1]{1,0:T(8,128)S(1)}, f32[32,1]{1,0:T(8,128)S(1)}, u32[]{:S(2)}, u32[]{:S(2)}) collective-permute-start(f32[32,1]{1,0:T(8,128)S(1)} %get-tuple-element.153), channel_id=1, source_target_pairs={{4,0},{8,4},{12,8},{0,12},{5,1},{9,5},{13,9},{1,13},{6,2},{10,6},{... | collective-permute-start | bytes 392 | tf_op jit(solution)/shard_map/ppermute | solution.py:25
  7.4 6.0 collective-permute-start.13
  7.6 7.7 %collective-permute-start.1 = (f32[4,32,1]{2,1,0:T(8,128)S(1)}, f32[4,32,1]{2,1,0:T(8,128)S(1)}, u32[]{:S(2)}, u32[]{:S(2)}) collective-permute-start(f32[4,32,1]{2,1,0:T(8,128)S(1)} %get-tuple-element.87), channel_id=1, source_target_pairs={{4,0},{8,4},{12,8},{0,12},{5,1},{9,5},{13,9},{1,13},{6,2},{10,6},{... | collective-permute-start | bytes 1544 | tf_op jit(solution)/shard_map/ppermute | solution.py:25
  9.3 6.0 collective-permute-start
  9.4 7.8 %collective-permute-start.32 = (f32[1,32,1]{2,1,0:T(8,128)S(1)}, f32[1,32,1]{2,1,0:T(8,128)S(1)}, u32[]{:S(2)}, u32[]{:S(2)}) collective-permute-start(f32[1,32,1]{2,1,0:T(8,128)S(1)} %get-tuple-element.145), channel_id=1, source_target_pairs={{4,0},{8,4},{12,8},{0,12},{5,1},{9,5},{13,9},{1,13},{6,2},{10,6},{... | collective-permute-start | bytes 392 | tf_op jit(solution)/shard_map/ppermute | solution.py:25
  13.4 7.4 %collective-permute-start.33 = (f32[1,32,1]{2,1,0:T(8,128)S(1)}, f32[1,32,1]{2,1,0:T(8,128)S(1)}, u32[]{:S(2)}, u32[]{:S(2)}) collective-permute-start(f32[1,32,1]{2,1,0:T(8,128)S(1)} %get-tuple-element.144), channel_id=1, source_target_pairs={{0,4},{4,8},{8,12},{12,0},{1,5},{5,9},{9,13},{13,1},{2,6},{6,10},{... | collective-permute-start | bytes 392 | tf_op jit(solution)/shard_map/ppermute | solution.py:24
  13.5 204.0 %collective-permute-start.4 = (f32[32,32,1]{2,1,0:T(8,128)}, f32[32,32,1]{2,1,0:T(8,128)S(1)}, u32[]{:S(2)}, u32[]{:S(2)}) collective-permute-start(f32[32,32,1]{2,1,0:T(8,128)} %get-tuple-element.79), channel_id=1, source_target_pairs={{4,0},{8,4},{12,8},{0,12},{5,1},{9,5},{13,9},{1,13},{6,2},{10,6},{... | collective-permute-start | bytes 12296 | tf_op jit(solution)/shard_map/ppermute | solution.py:25
  15.3 202.7 %collective-permute-start.5 = (f32[32,32,1]{2,1,0:T(8,128)}, f32[32,32,1]{2,1,0:T(8,128)S(1)}, u32[]{:S(2)}, u32[]{:S(2)}) collective-permute-start(f32[32,32,1]{2,1,0:T(8,128)} %get-tuple-element.78), channel_id=1, source_target_pairs={{0,4},{4,8},{8,12},{12,0},{1,5},{5,9},{9,13},{13,1},{2,6},{6,10},{... | collective-permute-start | bytes 12296 | tf_op jit(solution)/shard_map/ppermute | solution.py:24
  15.3 198.7 %collective-permute-start.8 = (f32[32,32,1]{2,1,0:T(8,128)}, f32[32,32,1]{2,1,0:T(8,128)}, u32[]{:S(2)}, u32[]{:S(2)}) collective-permute-start(f32[32,32,1]{2,1,0:T(8,128)} %get-tuple-element.77), channel_id=1, source_target_pairs={{4,0},{8,4},{12,8},{0,12},{5,1},{9,5},{13,9},{1,13},{6,2},{10,6},{... | collective-permute-start | bytes 12296 | tf_op jit(solution)/shard_map/ppermute | solution.py:25
  20.8 5.4 collective-permute-start.2
  22.1 5.6 collective-permute-start.15
  209.9 12.3 %collective-permute-start.9 = (f32[32,32,1]{2,1,0:T(8,128)}, f32[32,32,1]{2,1,0:T(8,128)S(1)}, u32[]{:S(2)}, u32[]{:S(2)}) collective-permute-start(f32[32,32,1]{2,1,0:T(8,128)} %get-tuple-element.76), channel_id=1, source_target_pairs={{0,4},{4,8},{8,12},{12,0},{1,5},{5,9},{9,13},{13,1},{2,6},{6,10},{... | collective-permute-start | bytes 12296 | tf_op jit(solution)/shard_map/ppermute | solution.py:24
  211.7 12.7 %collective-permute-start.27 = (f32[1,1,130]{2,1,0:T(1,128)S(1)}, f32[1,1,130]{2,1,0:T(1,128)S(1)}, u32[]{:S(2)}, u32[]{:S(2)}) collective-permute-start(f32[1,1,130]{2,1,0:T(1,128)S(1)} %get-tuple-element.107), channel_id=1, source_target_pairs={{0,1},{1,2},{2,3},{3,0},{4,5},{5,6},{6,7},{7,4},{8,9},{9,10},{10,1... | collective-permute-start | bytes 1568 | tf_op jit(solution)/shard_map/ppermute | solution.py:24
  214.0 14.0 %collective-permute-start.26 = (f32[1,1,130]{2,1,0:T(1,128)S(1)}, f32[1,1,130]{2,1,0:T(1,128)S(1)}, u32[]{:S(2)}, u32[]{:S(2)}) collective-permute-start(f32[1,1,130]{2,1,0:T(1,128)S(1)} %get-tuple-element.106), channel_id=1, source_target_pairs={{1,0},{2,1},{3,2},{0,3},{5,4},{6,5},{7,6},{4,7},{9,8},{10,9},{11,1... | collective-permute-start | bytes 1568 | tf_op jit(solution)/shard_map/ppermute | solution.py:25
  217.5 11.2 %collective-permute-start.43 = (f32[1,1,130]{2,1,0:T(1,128)S(1)}, f32[1,1,130]{2,1,0:T(1,128)S(1)}, u32[]{:S(2)}, u32[]{:S(2)}) collective-permute-start(f32[1,1,130]{2,1,0:T(1,128)S(1)} %get-tuple-element.105), channel_id=1, source_target_pairs={{0,1},{1,2},{2,3},{3,0},{4,5},{5,6},{6,7},{7,4},{8,9},{9,10},{10,1... | collective-permute-start | bytes 1568 | tf_op jit(solution)/shard_map/ppermute | solution.py:24
  218.0 10.8 %collective-permute-start.42 = (f32[1,1,130]{2,1,0:T(1,128)S(1)}, f32[1,1,130]{2,1,0:T(1,128)S(1)}, u32[]{:S(2)}, u32[]{:S(2)}) collective-permute-start(f32[1,1,130]{2,1,0:T(1,128)S(1)} %get-tuple-element.104), channel_id=1, source_target_pairs={{1,0},{2,1},{3,2},{0,3},{5,4},{6,5},{7,6},{4,7},{9,8},{10,9},{11,1... | collective-permute-start | bytes 1568 | tf_op jit(solution)/shard_map/ppermute | solution.py:25
  222.2 139.3 %collective-permute-start.7 = (f32[32,1,130]{2,1,0:T(1,128)}, f32[32,1,130]{2,1,0:T(1,128)}, u32[]{:S(2)}, u32[]{:S(2)}) collective-permute-start(f32[32,1,130]{2,1,0:T(1,128)} %get-tuple-element.70), channel_id=1, source_target_pairs={{0,1},{1,2},{2,3},{3,0},{4,5},{5,6},{6,7},{7,4},{8,9},{9,10},{10,1... | collective-permute-start | bytes 49928 | tf_op jit(solution)/shard_map/ppermute | solution.py:24
  224.3 137.2 %collective-permute-start.6 = (f32[32,1,130]{2,1,0:T(1,128)}, f32[32,1,130]{2,1,0:T(1,128)S(1)}, u32[]{:S(2)}, u32[]{:S(2)}) collective-permute-start(f32[32,1,130]{2,1,0:T(1,128)} %get-tuple-element.69), channel_id=1, source_target_pairs={{1,0},{2,1},{3,2},{0,3},{5,4},{6,5},{7,6},{4,7},{9,8},{10,9},{11,1... | collective-permute-start | bytes 49928 | tf_op jit(solution)/shard_map/ppermute | solution.py:25
  228.0 133.5 %collective-permute-start.11 = (f32[32,1,130]{2,1,0:T(1,128)}, f32[32,1,130]{2,1,0:T(1,128)S(1)}, u32[]{:S(2)}, u32[]{:S(2)}) collective-permute-start(f32[32,1,130]{2,1,0:T(1,128)} %get-tuple-element.68), channel_id=1, source_target_pairs={{0,1},{1,2},{2,3},{3,0},{4,5},{5,6},{6,7},{7,4},{8,9},{9,10},{10,1... | collective-permute-start | bytes 49928 | tf_op jit(solution)/shard_map/ppermute | solution.py:24
  355.2 5.4 collective-permute-start.51
  355.2 5.4 collective-permute-start.50
  372.8 5.4 collective-permute-start.59
  448.6 5.4 collective-permute-start.63
  600.0 5.4 collective-permute-start.71
  604.9 44.9 %collective-permute-start.53 = (f32[32,32,1]{2,1,0:T(8,128)}, f32[32,32,1]{2,1,0:T(8,128)}, u32[]{:S(2)}, u32[]{:S(2)}) collective-permute-start(f32[32,32,1]{2,1,0:T(8,128)} %get-tuple-element.74), channel_id=1, source_target_pairs={{0,4},{4,8},{8,12},{12,0},{1,5},{5,9},{9,13},{13,1},{2,6},{6,10},{... | collective-permute-start | bytes 12296 | tf_op jit(solution)/shard_map/ppermute | solution.py:24
  640.8 9.1 %collective-permute-start.52 = (f32[32,32,1]{2,1,0:T(8,128)}, f32[32,32,1]{2,1,0:T(8,128)S(1)}, u32[]{:S(2)}, u32[]{:S(2)}) collective-permute-start(f32[32,32,1]{2,1,0:T(8,128)} %get-tuple-element.73), channel_id=1, source_target_pairs={{4,0},{8,4},{12,8},{0,12},{5,1},{9,5},{13,9},{1,13},{6,2},{10,6},{... | collective-permute-start | bytes 12296 | tf_op jit(solution)/shard_map/ppermute | solution.py:25
  647.6 11.7 %collective-permute-start.76 = (f32[32,32,1]{2,1,0:T(8,128)S(1)}, f32[32,32,1]{2,1,0:T(8,128)S(1)}, u32[]{:S(2)}, u32[]{:S(2)}) collective-permute-start(f32[32,32,1]{2,1,0:T(8,128)S(1)} %get-tuple-element.72), channel_id=1, source_target_pairs={{4,0},{8,4},{12,8},{0,12},{5,1},{9,5},{13,9},{1,13},{6,2},{10,6},{... | collective-permute-start | bytes 12296 | tf_op jit(solution)/shard_map/ppermute | solution.py:25
  648.9 12.1 %collective-permute-start.77 = (f32[32,32,1]{2,1,0:T(8,128)S(1)}, f32[32,32,1]{2,1,0:T(8,128)S(1)}, u32[]{:S(2)}, u32[]{:S(2)}) collective-permute-start(f32[32,32,1]{2,1,0:T(8,128)S(1)} %get-tuple-element.71), channel_id=1, source_target_pairs={{0,4},{4,8},{8,12},{12,0},{1,5},{5,9},{9,13},{13,1},{2,6},{6,10},{... | collective-permute-start | bytes 12296 | tf_op jit(solution)/shard_map/ppermute | solution.py:24
  651.3 16.5 %collective-permute-start.55 = (f32[32,1,130]{2,1,0:T(1,128)S(1)}, f32[32,1,130]{2,1,0:T(1,128)S(1)}, u32[]{:S(2)}, u32[]{:S(2)}) collective-permute-start(f32[32,1,130]{2,1,0:T(1,128)S(1)} %get-tuple-element.66), channel_id=1, source_target_pairs={{0,1},{1,2},{2,3},{3,0},{4,5},{5,6},{6,7},{7,4},{8,9},{9,10},{10,1... | collective-permute-start | bytes 49928 | tf_op jit(solution)/shard_map/ppermute | solution.py:24
  651.9 16.0 %collective-permute-start.54 = (f32[32,1,130]{2,1,0:T(1,128)S(1)}, f32[32,1,130]{2,1,0:T(1,128)S(1)}, u32[]{:S(2)}, u32[]{:S(2)}) collective-permute-start(f32[32,1,130]{2,1,0:T(1,128)S(1)} %get-tuple-element.65), channel_id=1, source_target_pairs={{1,0},{2,1},{3,2},{0,3},{5,4},{6,5},{7,6},{4,7},{9,8},{10,9},{11,1... | collective-permute-start | bytes 49928 | tf_op jit(solution)/shard_map/ppermute | solution.py:25
  661.3 9.0 %collective-permute-start.79 = (f32[32,1,130]{2,1,0:T(1,128)S(1)}, f32[32,1,130]{2,1,0:T(1,128)S(1)}, u32[]{:S(2)}, u32[]{:S(2)}) collective-permute-start(f32[32,1,130]{2,1,0:T(1,128)S(1)} %get-tuple-element.64), channel_id=1, source_target_pairs={{0,1},{1,2},{2,3},{3,0},{4,5},{5,6},{6,7},{7,4},{8,9},{9,10},{10,1... | collective-permute-start | bytes 49928 | tf_op jit(solution)/shard_map/ppermute | solution.py:24
  661.9 8.4 %collective-permute-start.78 = (f32[32,1,130]{2,1,0:T(1,128)S(1)}, f32[32,1,130]{2,1,0:T(1,128)S(1)}, u32[]{:S(2)}, u32[]{:S(2)}) collective-permute-start(f32[32,1,130]{2,1,0:T(1,128)S(1)} %get-tuple-element.63), channel_id=1, source_target_pairs={{1,0},{2,1},{3,2},{0,3},{5,4},{6,5},{7,6},{4,7},{9,8},{10,9},{11,1... | collective-permute-start | bytes 49928 | tf_op jit(solution)/shard_map/ppermute | solution.py:25
  (79 other events, 698.2 us)
where the time goes:
time: 679 us; the launch traced here: 676 us
  blocking collectives  443 us (65%)
  starting transfers between devices  89.1 us (13%)
  other arithmetic  57.9 us (9%)
  waiting for transfers between devices  48.6 us (7%)
  between operations  29.3 us (4%)
  local copies, waits for them, and re-layouts  8.04 us (1%)
    psum x8, blocking collectives, squares(): return lax.psum(member_sum(residual * residual), ('lon', 'lat'))  249 us
    psum x6, blocking collectives, poisson_inversion(): curve = lax.psum(member_sum(direction * image), ('lon', 'lat'))  194 us
    ppermute x40, starting transfers between devices, extended(): after = lax.ppermute(initial, axis, down)  67.7 us
    ppermute x40, waiting for transfers between devices, extended(): before = lax.ppermute(last, axis, up)  31.3 us
    ppermute x40, starting transfers between devices, extended(): before = lax.ppermute(last, axis, up)  21.4 us
    reduce_sum x23, other arithmetic, member_sum(): return jnp.sum(field, axis=(1, 2))  21.4 us
    ppermute x40, waiting for transfers between devices, extended(): after = lax.ppermute(initial, axis, down)  17.4 us
  transfers between devices with their start and end apart: 80, of which 38 were waited for; matrix products, arithmetic and copies ran while one was open for 7% of the time, Pallas kernels for 0%

commit v1 on v0

v1 whole, which is shorter than its diff:
```python
import functools
import math

import jax
import jax.numpy as jnp
from jax import lax
from jax.experimental import pallas as pl
from jax.experimental.pallas import tpu as pltpu
from jax.sharding import PartitionSpec as P

EOS_QUAD = 0.1
PRESS_COEF = 0.5
SURF_COEF = 4.0
COUPLING = 1.0

MESH = pl.DeviceIdType.MESH
RIM = 8
STEP = 4
SHIFT = 1.2
LINK = 0.2
ENTRIES = 11
WAYS = ((1, 0), (-1, 0), (0, 1), (0, -1), (1, 1), (-1, 1), (1, -1), (-1, -1))
BACK = tuple(WAYS.index((-a, -b)) for a, b in WAYS)


def rolled(x, shift, axis):
    return pltpu.roll(x, shift % x.shape[axis], axis)


def kernel(
    heat_hbm, height, closing_hbm, closing_height, mixing, sea, layers,
    out_ref, surface_ref, diff_ref,
    heat_v, closing_v, m0_v, t1_v, u_v, m1_v, w2,
    mine_a, ew_a, d_a, mine_b, ew_b, d_b, mine_c, ew_c, d_c,
    pack_1, rp_1, row_1n, row_1s, rr_1, pack_2, rp_2, row_2n, row_2s, rr_2,
    vec_0, slots_0, vec_1, slots_1, vec_2, slots_2,
    load_sem, send_h, recv_h, send_p, recv_p, send_g, recv_g,
):
    levels, rows, lanes = heat_v.shape
    n_lon, n_lat = lax.axis_size("lon"), lax.axis_size("lat")
    group = n_lon * n_lat
    lon, lat = lax.axis_index("lon"), lax.axis_index("lat")
    me = lat * n_lon + lon

    heat_load = pltpu.make_async_copy(heat_hbm, heat_v, load_sem.at[0])
    closing_load = pltpu.make_async_copy(closing_hbm, closing_v, load_sem.at[1])
    heat_load.start()
    closing_load.start()

    def peer(index):
        return {"lon": lax.rem(index, n_lon), "lat": lax.div(index, n_lon)}

    barrier = pltpu.get_barrier_semaphore()

    def greet(step, carry):
        pl.semaphore_signal(
            barrier, inc=1, device_id=peer(lax.rem(me + step, group)), device_id_type=MESH
        )
        return carry

    lax.fori_loop(1, group, greet, 0)

    def there(way):
        if WAYS[way][1] == 1:
            return lat < n_lat - 1
        if WAYS[way][1] == -1:
            return lat > 0
        return None

    def when(cond, action):
        if cond is None:
            action()
        else:
            pl.when(cond)(action)

    def target(way):
        return {
            "lon": lax.rem(lon + WAYS[way][0] + n_lon, n_lon),
            "lat": lat + WAYS[way][1],
        }

    def clear_south():
        for ref in (d_a, d_b, d_c):
            for slot in (1, 4, 5):
                ref[slot] = jnp.zeros(ref.shape[1:], jnp.float32)
        for ref in (rr_1, rr_2):
            ref[1] = jnp.zeros(ref.shape[1:], jnp.float32)

    def clear_north():
        for ref in (d_a, d_b, d_c):
            for slot in (0, 2, 3):
                ref[slot] = jnp.zeros(ref.shape[1:], jnp.float32)
        for ref in (rr_1, rr_2):
            ref[0] = jnp.zeros(ref.shape[1:], jnp.float32)

    pl.when(lat == 0)(clear_south)
    pl.when(lat == n_lat - 1)(clear_north)

    def halo(mine, ew, d, turn):
        copies = []
        for way in range(8):
            slot = BACK[way]
            if way < 2:
                src, dst = mine, ew.at[slot]
            else:
                first = rows - RIM if WAYS[way][1] == 1 else 0
                src, dst = mine.at[:, pl.ds(first, RIM), :], d.at[slot - 2]
            copies.append(
                pltpu.make_async_remote_copy(
                    src_ref=src,
                    dst_ref=dst,
                    send_sem=send_h.at[turn * 8 + way],
                    recv_sem=recv_h.at[turn * 8 + slot],
                    device_id=target(way),
                    device_id_type=MESH,
                )
            )
        return copies

    def columns(pack, rp, row_n, row_s, rr, turn):
        copies = []
        for way in range(4):
            slot = BACK[way]
            src = (pack, pack, row_n, row_s)[way]
            dst = rp.at[slot] if way < 2 else rr.at[slot - 2]
            copies.append(
                pltpu.make_async_remote_copy(
                    src_ref=src,
                    dst_ref=dst,
                    send_sem=send_p.at[turn * 4 + way],
                    recv_sem=recv_p.at[turn * 4 + slot],
                    device_id=target(way),
                    device_id_type=MESH,
                )
            )
        return copies

    def start(copies):
        for way, copy in enumerate(copies):
            when(there(way), copy.start)

    def arrive(copies):
        for way, copy in enumerate(copies):
            when(there(BACK[way]), copy.wait_recv)

    def sent(copies):
        for way, copy in enumerate(copies):
            when(there(way), copy.wait_send)

    def share(vec, slots, turn):
        def one(step, carry):
            pltpu.make_async_remote_copy(
                src_ref=vec,
                dst_ref=slots.at[me],
                send_sem=send_g.at[turn],
                recv_sem=recv_g.at[turn],
                device_id=peer(lax.rem(me + step, group)),
                device_id_type=MESH,
            ).start()
            return carry

        slots[me] = vec[...]
        lax.fori_loop(1, group, one, 0)

    def shared(slots, sem, turn):
        several = slots.at[pl.ds(0, group - 1)]
        pltpu.make_async_copy(several, several, sem.at[turn]).wait()

    halo_a = halo(mine_a, ew_a, d_a, 0)
    halo_b = halo(mine_b, ew_b, d_b, 1)
    halo_c = halo(mine_c, ew_c, d_c, 2)
    cols_1 = columns(pack_1, rp_1, row_1n, row_1s, rr_1, 0)
    cols_2 = columns(pack_2, rp_2, row_2n, row_2s, rr_2, 1)

    lane = lax.broadcasted_iota(jnp.int32, (rows, lanes), 1)
    row = lax.broadcasted_iota(jnp.int32, (rows, lanes), 0)
    lane_8 = lax.broadcasted_iota(jnp.int32, (8, lanes), 1)
    sub_8 = lax.broadcasted_iota(jnp.int32, (8, lanes), 0)

    code = (sea[...] * layers[...]).astype(jnp.float32)
    mine_a[0] = code
    mine_a[1] = mixing[...]
    mine_a[2] = height[...]

    def folded(x):
        total = x[0:8]
        for i in range(8, x.shape[0], 8):
            total = total + x[i : i + 8]
        return jnp.sum(total, axis=0, keepdims=True)

    def gathered(sums, places):
        result = jnp.zeros((1, lanes), jnp.float32)
        for first in range(0, len(sums), 8):
            some = sums[first : first + 8]
            table = jnp.zeros((8, lanes), jnp.float32)
            spot = jnp.full((8, lanes), -1, jnp.int32)
            for i, item in enumerate(some):
                table = jnp.where(sub_8 == i, item, table)
                spot = jnp.where(sub_8 == i, places[first + i], spot)
            column = jnp.sum(table, axis=1, keepdims=True)
            result = result + jnp.sum(
                jnp.where(lane_8 == spot, column, 0.0), axis=0, keepdims=True
            )
        return result

    share_of = code * (SURF_COEF / levels)
    east = jnp.minimum(share_of, rolled(share_of, -1, 1))
    north = jnp.minimum(share_of, rolled(share_of, -1, 0))
    diagonal = east + rolled(east, 1, 1) + north + rolled(north, 1, 0)
    second_moment = diagonal * diagonal + 2.0 * (east * east + north * north)
    vec_0[...] = gathered([folded(diagonal), folded(second_moment)], [0, 1])

    pl.semaphore_wait(barrier, group - 1)
    start(halo_a)
    share(vec_0, slots_0, 0)

    heat_load.wait()
    closing_load.wait()

    def level_of(k):
        return k.astype(jnp.float32)

    def load_body(block, carry):
        press, total = carry
        for i in range(STEP):
            k = block * STEP + i
            kf = level_of(k)
            h = heat_v[k]
            wet = code > kf
            masked = jnp.where(wet, closing_v[k], 0.0)
            m0_v[k] = masked
            press = press + jnp.where(
                wet, (kf + 0.5) / levels * (h + EOS_QUAD * h * h), 0.0
            )
            total = total + COUPLING * (1.0 - kf / levels) * masked
        return press, total

    zero = jnp.zeros((rows, lanes), jnp.float32)
    press, total_one = lax.fori_loop(
        0, levels // STEP, load_body, (zero, closing_height[...])
    )
    mine_b[0] = press / math.sqrt(levels)
    mine_b[1] = total_one
    start(halo_b)

    def packing(first_v, second_v, pack, row_n, row_s):
        def body(block, packed):
            for i in range(STEP):
                k = block * STEP + i
                a = first_v[k]
                b = second_v[k]
                packed = jnp.where((lane >> 1) == k, pltpu.roll(a, 2 * k + 1, 1), packed)
                packed = jnp.where(
                    (lane >> 1) == k + levels,
                    pltpu.roll(b, 2 * k + 2 * levels + 1, 1),
                    packed,
                )
                row_n[pl.ds(k, 1), :] = a[rows - 1 : rows, :]
                row_n[pl.ds(k + levels, 1), :] = b[rows - 1 : rows, :]
                row_s[pl.ds(k, 1), :] = a[0:1, :]
                row_s[pl.ds(k + levels, 1), :] = b[0:1, :]
            return packed

        pack[...] = lax.fori_loop(0, levels // STEP, body, zero)

    packing(heat_v, m0_v, pack_1, row_1n, row_1s)
    start(cols_1)

    def wide(mine, ew, d, f):
        half = lax.broadcasted_iota(jnp.int32, (rows, lanes), 1) < lanes // 2
        half_8 = lax.broadcasted_iota(jnp.int32, (RIM, lanes), 1) < lanes // 2
        left = jnp.concatenate([mine[f], d[0, f], d[1, f]], axis=0)
        right = jnp.concatenate(
            [
                jnp.where(half, ew[0, f], ew[1, f]),
                jnp.where(half_8, d[2, f], d[3, f]),
                jnp.where(half_8, d[4, f], d[5, f]),
            ],
            axis=0,
        )
        return jnp.concatenate([left, right], axis=1)

    def own(x):
        return x[:rows, :lanes]

    def sides(x):
        return rolled(x, -1, 1), rolled(x, 1, 1), rolled(x, -1, 0), rolled(x, 1, 0)

    arrive(halo_a)
    code_w = wide(mine_a, ew_a, d_a, 0)
    mix_w = wide(mine_a, ew_a, d_a, 1)
    height_w = wide(mine_a, ew_a, d_a, 2)
    near_code = [jnp.minimum(code_w, x) for x in sides(code_w)]
    for i, x in enumerate(near_code):
        w2[i] = own(x)
    for i, x in enumerate(sides(mix_w)):
        w2[4 + i] = own(0.5 * (mix_w + x))
    face_land = [jnp.where(x > 0.0, 1.0, 0.0) for x in near_code]
    for i, x in enumerate(face_land):
        w2[8 + i] = own(x) * PRESS_COEF

    def totals(slots):
        return jnp.broadcast_to(jnp.sum(slots[...], axis=0), (8, lanes))

    def at(total, entry):
        return pltpu.roll(total, (lanes - entry) % lanes, 1)

    def scalar(x):
        return x[0:1, 0:1]

    shared(slots_0, recv_g, 0)
    moments = totals(slots_0)
    trace = at(moments, 0)
    ratio = jnp.where(trace > 0.0, at(moments, 1) / jnp.where(trace > 0.0, trace, 1.0), 1.0)
    scale = jnp.where(lane_8 < lanes // 2, ratio, pltpu.roll(ratio, lanes // 2, 1))
    weight = scalar(1.0 / scale) * (SURF_COEF / levels)
    solver_w = [x * weight for x in near_code]

    def apply(v):
        around = sides(v)
        result = solver_w[0] * (v - around[0])
        for w, x in zip(solver_w[1:], around[1:]):
            result = result + w * (v - x)
        return result

    def basis(b):
        v1 = apply(b)
        v2 = apply(v1) - SHIFT * v1
        v3 = apply(v2) - SHIFT * v2 - LINK * v1
        v4 = own(apply(v3))
        o = [own(v) for v in (b, v1, v2, v3)]
        pairs = ((0, 0), (0, 1), (0, 2), (0, 3), (1, 1), (1, 2), (1, 3), (2, 2), (2, 3), (3, 3))
        sums = [folded(o[i] * o[j]) for i, j in pairs] + [folded(o[3] * v4)]
        return (b, v1, v2, v3), sums

    def coefficients(total):
        g00, g01, g02, g03, g11, g12, g13, g22, g23, g33, g34 = [
            at(total, e) for e in range(ENTRIES)
        ]
        m = {
            (0, 0): g00 + scale * g01,
            (0, 1): g01 + scale * g11,
            (0, 2): g02 + scale * g12,
            (0, 3): g03 + scale * g13,
            (1, 1): g11 + scale * (g12 + SHIFT * g11),
            (1, 2): g12 + scale * (g22 + SHIFT * g12),
            (1, 3): g13 + scale * (g23 + SHIFT * g13),
            (2, 2): g22 + scale * (g23 + SHIFT * g22 + LINK * g12),
            (2, 3): g23 + scale * (g33 + SHIFT * g23 + LINK * g13),
            (3, 3): g33 + scale * g34,
        }
        c = [g00, g01, g02, g03]
        low, inverse = {}, []
        work = dict(m)
        for j in range(4):
            pivot = work[j, j]
            good = pivot > 3e-7 * m[j, j]
            inv = jnp.where(good, 1.0 / jnp.where(good, pivot, 1.0), 0.0)
            inverse.append(inv)
            for i in range(j + 1, 4):
                low[i, j] = work[j, i] * inv
            for i in range(j + 1, 4):
                for k in range(i, 4):
                    work[i, k] = work[i, k] - low[i, j] * work[j, k]
                c[i] = c[i] - low[i, j] * c[j]
        c = [x * inv for x, inv in zip(c, inverse)]
        for i in (2, 1, 0):
            for j in range(i + 1, 4):
                c[i] = c[i] - low[j, i] * c[j]
        return c

    def combined(c, vs):
        result = scalar(c[0]) * vs[0]
        for a, v in zip(c[1:], vs[1:]):
            result = result + scalar(a) * v
        return result

    def pressed(x):
        around = sides(x)
        centre = own(x)
        result = w2[8] * (centre - own(around[0]))
        for i in range(1, 4):
            result = result + w2[8 + i] * (centre - own(around[i]))
        return result * (1.0 / math.sqrt(levels))

    arrive(halo_b)
    press_w = wide(mine_b, ew_b, d_b, 0)
    rhs = height_w
    for w, x in zip(face_land, sides(press_w)):
        rhs = rhs + (PRESS_COEF * w) * (press_w - x)
    basis_1, sums_1 = basis(rhs)
    basis_2, sums_2 = basis(wide(mine_b, ew_b, d_b, 1))
    half = lanes // 2
    vec_1[...] = gathered(
        sums_1 + sums_2, list(range(ENTRIES)) + [half + e for e in range(ENTRIES)]
    )
    share(vec_1, slots_1, 1)

    def mixed(rp):
        return jnp.where((lane & 1) == 0, rolled(rp[0], -1, 1), rolled(rp[1], 1, 1))

    def around_of(v, rim, shift, rr, k):
        r = pltpu.roll(rim, shift, 1)
        return (
            jnp.where(lane == lanes - 1, r, rolled(v, -1, 1)),
            jnp.where(lane == 0, r, rolled(v, 1, 1)),
            jnp.where(row == rows - 1, rr[0, pl.ds(k, 1), :], rolled(v, -1, 0)),
            jnp.where(row == 0, rr[1, pl.ds(k, 1), :], rolled(v, 1, 0)),
        )

    arrive(cols_1)
    w2[12] = mixed(rp_1)

    def diffuse_body(block, carry):
        rim = w2[12]
        for i in range(2):
            k = block * 2 + i
            kf = level_of(k)
            h = heat_v[k]
            m = m0_v[k]
            h_around = around_of(h, rim, 127 - 2 * k, rr_1, k)
            m_around = around_of(m, rim, 127 - 2 * levels - 2 * k, rr_1, k + levels)
            h_sum, m_sum = h, m
            for f in range(4):
                w = jnp.where(w2[f] > kf, w2[4 + f], 0.0)
                h_sum = h_sum + w * (h_around[f] - h)
                m_sum = m_sum + w * (m_around[f] - m)
            t1_v[k] = jnp.where(code > kf, h_sum, 0.0)
            u_v[k] = m_sum
        return carry

    lax.fori_loop(0, levels // 2, diffuse_body, 0)

    shared(slots_1, recv_g, 1)
    coef = coefficients(totals(slots_1))
    surface_next = combined(coef, [own(v) for v in basis_1])
    back_one = combined([pltpu.roll(c, half, 1) for c in coef], basis_2)
    back_press = pressed(back_one)

    def reverse_body(block, total):
        for i in range(STEP):
            k = block * STEP + i
            kf = level_of(k)
            wet = code > kf
            second = t1_v[k] + jnp.where(
                wet, COUPLING * (1.0 - kf / levels) * surface_next, 0.0
            )
            t1_v[k] = second
            masked = jnp.where(
                wet,
                u_v[k]
                + (kf + 0.5) / levels * (1.0 + 2.0 * EOS_QUAD * second) * back_press,
                0.0,
            )
            m1_v[k] = masked
            total = total + COUPLING * (1.0 - kf / levels) * masked
        return total

    mine_c[0] = lax.fori_loop(0, levels // STEP, reverse_body, own(back_one))
    start(halo_c)
    packing(t1_v, m1_v, pack_2, row_2n, row_2s)
    start(cols_2)

    arrive(halo_c)
    basis_3, sums_3 = basis(wide(mine_c, ew_c, d_c, 0))
    vec_2[...] = gathered(sums_3, list(range(ENTRIES)))
    share(vec_2, slots_2, 2)

    arrive(cols_2)
    w2[13] = mixed(rp_2)

    def gradient_body(k, total):
        kf = level_of(k)
        h, m0, t, m1 = heat_v[k], m0_v[k], t1_v[k], m1_v[k]
        shift = 127 - 2 * k
        far = shift - 2 * levels
        h_around = around_of(h, w2[12], shift, rr_1, k)
        m0_around = around_of(m0, w2[12], far, rr_1, k + levels)
        t_around = around_of(t, w2[13], shift, rr_2, k)
        m1_around = around_of(m1, w2[13], far, rr_2, k + levels)
        spread = m1
        for f in range(4):
            wet = w2[f] > kf
            step = m1_around[f] - m1
            spread = spread + jnp.where(wet, w2[4 + f], 0.0) * step
            total = total + jnp.where(
                wet, (h_around[f] - h) * step + (t_around[f] - t) * (m0_around[f] - m0), 0.0
            )
        u_v[k] = spread
        return total

    diff_ref[...] = -0.5 * lax.fori_loop(0, levels, gradient_body, zero)

    shared(slots_2, recv_g, 2)
    surface = combined(coefficients(totals(slots_2)), basis_3)
    surface_ref[...] = own(surface)
    last_press = pressed(surface)

    def final_body(block, carry):
        for i in range(STEP):
            k = block * STEP + i
            kf = level_of(k)
            out_ref[k] = u_v[k] + jnp.where(
                code > kf,
                (kf + 0.5) / levels * (1.0 + 2.0 * EOS_QUAD * heat_v[k]) * last_press,
                0.0,
            )
        return carry

    lax.fori_loop(0, levels // STEP, final_body, 0)

    for copies in (halo_a, halo_b, halo_c, cols_1, cols_2):
        sent(copies)
    for turn, slots in enumerate((slots_0, slots_1, slots_2)):
        shared(slots, send_g, turn)


def shards(group, *args):
    heat, height = args[0], args[1]
    levels, rows, lanes = heat.shape
    f32 = jnp.float32
    cube = pltpu.VMEM((levels, rows, lanes), f32)

    def halos(fields):
        return [
            pltpu.VMEM((fields, rows, lanes), f32),
            pltpu.VMEM((2, fields, rows, lanes), f32),
            pltpu.VMEM((6, fields, RIM, lanes), f32),
        ]

    columns = [
        pltpu.VMEM((rows, lanes), f32),
        pltpu.VMEM((2, rows, lanes), f32),
        pltpu.VMEM((2 * levels, lanes), f32),
        pltpu.VMEM((2 * levels, lanes), f32),
        pltpu.VMEM((2, 2 * levels, lanes), f32),
    ]
    sums = [pltpu.VMEM((1, lanes), f32), pltpu.VMEM((group, 1, lanes), f32)]
    vmem = pl.BlockSpec(memory_space=pltpu.VMEM)
    hbm = pl.BlockSpec(memory_space=pl.ANY)
    return pl.pallas_call(
        kernel,
        out_shape=(
            jax.ShapeDtypeStruct(heat.shape, f32),
            jax.ShapeDtypeStruct(height.shape, f32),
            jax.ShapeDtypeStruct(height.shape, f32),
        ),
        in_specs=[hbm, vmem, hbm, vmem, vmem, vmem, vmem],
        out_specs=(vmem, vmem, vmem),
        scratch_shapes=[cube] * 6
        + [pltpu.VMEM((14, rows, lanes), f32)]
        + halos(3)
        + halos(2)
        + halos(1)
        + columns
        + columns
        + sums * 3
        + [
            pltpu.SemaphoreType.DMA((2,)),
            pltpu.SemaphoreType.DMA((24,)),
            pltpu.SemaphoreType.DMA((24,)),
            pltpu.SemaphoreType.DMA((8,)),
            pltpu.SemaphoreType.DMA((8,)),
            pltpu.SemaphoreType.DMA((3,)),
            pltpu.SemaphoreType.DMA((3,)),
        ],
        compiler_params=pltpu.CompilerParams(
            collective_id=0, has_side_effects=True, vmem_limit_bytes=40 * 1024 * 1024
        ),
    )(*args)


def solution(mesh):
    group = mesh.shape["lon"] * mesh.shape["lat"]
    cube = P(None, ("member", "lat"), "lon")
    plane = P(("member", "lat"), "lon")
    fixed = P("lat", "lon")
    return jax.shard_map(
        functools.partial(shards, group),
        mesh=mesh,
        in_specs=(cube, plane, cube, plane, fixed, fixed, fixed),
        out_specs=(cube, plane, plane),
        check_vma=False,
    )
```

time: 679 us -> 33.6 us (0.05)
  blocking collectives: 443 us -> 0 us
  starting transfers between devices: 89.1 us -> 0 us
  other arithmetic: 57.9 us -> 0 us
  waiting for transfers between devices: 48.6 us -> 0 us
  between operations: 29.3 us -> 0.66 us
  Pallas kernels: 0 us -> 24.6 us
    psum x14 -> x0, blocking collectives: 443 us -> none  [the longest x8 249 us: squares(): return lax.psum(member_sum(residual * residual), ('lon', 'lat'))]
    ppermute x80 -> x0, starting transfers between devices: 89.1 us -> none  [the longest x40 67.7 us: extended(): after = lax.ppermute(initial, axis, down)]
    ppermute x80 -> x0, waiting for transfers between devices: 48.6 us -> none  [the longest x40 31.3 us: extended(): before = lax.ppermute(last, axis, up)]
    reduce_sum x28 -> x0, other arithmetic: 35.6 us -> none  [the longest x23 21.4 us: member_sum(): return jnp.sum(field, axis=(1, 2))]
    pallas_call x0 -> x1, Pallas kernels: none -> 24.6 us  [shards(): pl.pallas_call(kernel, out_shape=(jax.ShapeDtypeStruct(heat.shape, f32),...]
    add x13 -> x0, other arithmetic: 8.42 us -> none  [the longest x9 3.68 us: poisson_inversion(): direction = residual + spread(norm_next / norm_now) * direction]
  transfers between devices with their start and end apart: 80 -> 0, of which waited for: 38 -> 0; matrix products, arithmetic and copies ran while one was open for 7% -> 0% of each run, Pallas kernels for 0% -> 0%
where the time goes in v1:
time: 33.6 us; the launch traced here: 33 us
  Pallas kernels  24.6 us (73%)
  local copies, waits for them, and re-layouts  7.67 us (23%)
  between operations  0.66 us (2%)
    pallas_call x1, Pallas kernels, shards(): pl.pallas_call(kernel, out_shape=(jax.ShapeDtypeStruct(heat.shape, f32),...  24.6 us
    unnamed x17, local copies, waits for them, and re-layouts  7.67 us

profile of v1, /device:TPU:0, one launch (start us, length us, event | category | flops | bytes accessed | tf_op | source)
XLA Modules:
  0.0 33.0 jit_solution(15185353128734398470)
XLA Ops:
  0.6 0.0 copy-start
  0.6 1.0 %copy-done = f32[32,32,128]{2,1,0:T(8,128)S(1)} copy-done((f32[32,32,128]{2,1,0:T(8,128)S(1)}, f32[32,32,128]{2,1,0:T(8,128)}, u32[]{:S(2)}) %copy-start) | copy-done | bytes 524312
  1.7 0.0 copy-start.1
  1.7 1.0 %copy-done.1 = f32[32,32,128]{2,1,0:T(8,128)S(1)} copy-done((f32[32,32,128]{2,1,0:T(8,128)S(1)}, f32[32,32,128]{2,1,0:T(8,128)}, u32[]{:S(2)}) %copy-start.1) | copy-done | bytes 524312
  2.7 0.0 copy-start.2
  2.7 0.7 %copy-done.2 = f32[32,128]{1,0:T(8,128)S(1)} copy-done((f32[32,128]{1,0:T(8,128)S(1)}, f32[32,128]{1,0:T(8,128)}, u32[]{:S(2)}) %copy-start.2) | copy-done | bytes 16408
  3.4 0.0 copy-start.3
  3.4 0.7 %copy-done.3 = f32[32,128]{1,0:T(8,128)S(1)} copy-done((f32[32,128]{1,0:T(8,128)S(1)}, f32[32,128]{1,0:T(8,128)}, u32[]{:S(2)}) %copy-start.3) | copy-done | bytes 16408
  4.2 0.0 copy-start.4
  4.2 0.7 %copy-done.4 = f32[32,128]{1,0:T(8,128)S(1)} copy-done((f32[32,128]{1,0:T(8,128)S(1)}, f32[32,128]{1,0:T(8,128)}, u32[]{:S(2)}) %copy-start.4) | copy-done | bytes 16408
  4.9 0.0 copy-start.5
  4.9 0.7 %copy-done.5 = s32[32,128]{1,0:T(8,128)S(1)} copy-done((s32[32,128]{1,0:T(8,128)S(1)}, s32[32,128]{1,0:T(8,128)}, u32[]{:S(2)}) %copy-start.5) | copy-done | bytes 16408
  5.6 0.0 copy-start.6
  5.6 0.7 %copy-done.6 = s32[32,128]{1,0:T(8,128)S(1)} copy-done((s32[32,128]{1,0:T(8,128)S(1)}, s32[32,128]{1,0:T(8,128)}, u32[]{:S(2)}) %copy-start.6) | copy-done | bytes 16408
  6.3 24.6 %shard_map.94 = (f32[32,32,128]{2,1,0:T(8,128)S(1)}, f32[32,128]{1,0:T(8,128)S(1)}, f32[32,128]{1,0:T(8,128)S(1)}) custom-call(f32[32,32,128]{2,1,0:T(8,128)S(1)} %copy-done, f32[32,128]{1,0:T(8,128)S(1)} %copy-done.2, f32[32,32,128]{2,1,0:T(8,128)S(1)} %copy-done.1, f32[32,128]{1,0:T(8,128)S(1)} %copy-done.3, f32[32,128]{1,0:T(8,128)S(1)} %copy-done.4, ...), custom_call_target="tpu_custom_call" | custom-call | tf_op jit(solution)/shard_map/pallas_call | solution.py:541
  30.9 0.8 %copy.13 = f32[32,32,128]{2,1,0:T(8,128)} copy(f32[32,32,128]{2,1,0:T(8,128)S(1)} %get-tuple-element.6) | data formatting | bytes 1048576
  31.7 0.6 %copy.14 = f32[32,128]{1,0:T(8,128)} copy(f32[32,128]{1,0:T(8,128)S(1)} %get-tuple-element.7) | data formatting | bytes 32768
  32.3 0.6 %copy.15 = f32[32,128]{1,0:T(8,128)} copy(f32[32,128]{1,0:T(8,128)S(1)} %get-tuple-element.8) | data formatting | bytes 32768
Async XLA Ops:
  0.6 1.0 %copy-start = (f32[32,32,128]{2,1,0:T(8,128)S(1)}, f32[32,32,128]{2,1,0:T(8,128)}, u32[]{:S(2)}) copy-start(f32[32,32,128]{2,1,0:T(8,128)} %heat_hbm.1) | copy-start | bytes 1572868
  1.7 1.0 %copy-start.1 = (f32[32,32,128]{2,1,0:T(8,128)S(1)}, f32[32,32,128]{2,1,0:T(8,128)}, u32[]{:S(2)}) copy-start(f32[32,32,128]{2,1,0:T(8,128)} %closing_hbm.1) | copy-start | bytes 1572868
  2.7 0.7 %copy-start.2 = (f32[32,128]{1,0:T(8,128)S(1)}, f32[32,128]{1,0:T(8,128)}, u32[]{:S(2)}) copy-start(f32[32,128]{1,0:T(8,128)} %height.1) | copy-start | bytes 49156
  3.4 0.7 %copy-start.3 = (f32[32,128]{1,0:T(8,128)S(1)}, f32[32,128]{1,0:T(8,128)}, u32[]{:S(2)}) copy-start(f32[32,128]{1,0:T(8,128)} %closing_height.1) | copy-start | bytes 49156
  4.2 0.7 %copy-start.4 = (f32[32,128]{1,0:T(8,128)S(1)}, f32[32,128]{1,0:T(8,128)}, u32[]{:S(2)}) copy-start(f32[32,128]{1,0:T(8,128)} %mixing.1) | copy-start | bytes 49156
  4.9 0.7 %copy-start.5 = (s32[32,128]{1,0:T(8,128)S(1)}, s32[32,128]{1,0:T(8,128)}, u32[]{:S(2)}) copy-start(s32[32,128]{1,0:T(8,128)} %sea.1) | copy-start | bytes 49156
  5.6 0.7 %copy-start.6 = (s32[32,128]{1,0:T(8,128)S(1)}, s32[32,128]{1,0:T(8,128)}, u32[]{:S(2)}) copy-start(s32[32,128]{1,0:T(8,128)} %layers.1) | copy-start | bytes 49156

commit v2 on v1

--- a/solution.py
+++ b/solution.py
@@ -14,7 +14,8 @@
 COUPLING = 1.0
 
 MESH = pl.DeviceIdType.MESH
-RIM = 8
+RIM = 16
+CHUNKS = 4
 STEP = 4
 SHIFT = 1.2
 LINK = 0.2
@@ -28,8 +29,9 @@
 
 
 def kernel(
-    heat_hbm, height, closing_hbm, closing_height, mixing, sea, layers,
+    heat_hbm, height_hbm, closing_hbm, closing_height_hbm, mixing_hbm, sea_hbm, layers_hbm,
     out_ref, surface_ref, diff_ref,
+    height, closing_height, mixing, sea, layers,
     heat_v, closing_v, m0_v, t1_v, u_v, m1_v, w2,
     mine_a, ew_a, d_a, mine_b, ew_b, d_b, mine_c, ew_c, d_c,
     pack_1, rp_1, row_1n, row_1s, rr_1, pack_2, rp_2, row_2n, row_2s, rr_2,
@@ -42,10 +44,32 @@
     lon, lat = lax.axis_index("lon"), lax.axis_index("lat")
     me = lat * n_lon + lon
 
-    heat_load = pltpu.make_async_copy(heat_hbm, heat_v, load_sem.at[0])
-    closing_load = pltpu.make_async_copy(closing_hbm, closing_v, load_sem.at[1])
-    heat_load.start()
-    closing_load.start()
+    loads = [
+        pltpu.make_async_copy(src, dst, load_sem.at[i])
+        for i, (src, dst) in enumerate(
+            (
+                (sea_hbm, sea),
+                (layers_hbm, layers),
+                (mixing_hbm, mixing),
+                (height_hbm, height),
+                (closing_height_hbm, closing_height),
+            )
+        )
+    ]
+    chunk = levels // CHUNKS
+    cube_loads = [
+        [
+            pltpu.make_async_copy(
+                src.at[pl.ds(c * chunk, chunk)],
+                dst.at[pl.ds(c * chunk, chunk)],
+                load_sem.at[5 + 2 * c + i],
+            )
+            for i, (src, dst) in enumerate(((heat_hbm, heat_v), (closing_hbm, closing_v)))
+        ]
+        for c in range(CHUNKS)
+    ]
+    for load in loads + sum(cube_loads, []):
+        load.start()
 
     def peer(index):
         return {"lon": lax.rem(index, n_lon), "lat": lax.div(index, n_lon)}
@@ -177,6 +201,8 @@
     lane_8 = lax.broadcasted_iota(jnp.int32, (8, lanes), 1)
     sub_8 = lax.broadcasted_iota(jnp.int32, (8, lanes), 0)
 
+    for load in loads[:4]:
+        load.wait()
     code = (sea[...] * layers[...]).astype(jnp.float32)
     mine_a[0] = code
     mine_a[1] = mixing[...]
@@ -214,8 +240,6 @@
     start(halo_a)
     share(vec_0, slots_0, 0)
 
-    heat_load.wait()
-    closing_load.wait()
 
     def level_of(k):
         return k.astype(jnp.float32)
@@ -236,34 +260,36 @@
         return press, total
 
     zero = jnp.zeros((rows, lanes), jnp.float32)
-    press, total_one = lax.fori_loop(
-        0, levels // STEP, load_body, (zero, closing_height[...])
-    )
+    loads[4].wait()
+    carry = (zero, closing_height[...])
+    for c in range(CHUNKS):
+        for load in cube_loads[c]:
+            load.wait()
+        first = c * chunk // STEP
+        carry = lax.fori_loop(first, first + chunk // STEP, load_body, carry)
+    press, total_one = carry
     mine_b[0] = press / math.sqrt(levels)
     mine_b[1] = total_one
     start(halo_b)
 
-    def packing(first_v, second_v, pack, row_n, row_s):
-        def body(block, packed):
-            for i in range(STEP):
-                k = block * STEP + i
-                a = first_v[k]
-                b = second_v[k]
-                packed = jnp.where((lane >> 1) == k, pltpu.roll(a, 2 * k + 1, 1), packed)
-                packed = jnp.where(
-                    (lane >> 1) == k + levels,
-                    pltpu.roll(b, 2 * k + 2 * levels + 1, 1),
-                    packed,
-                )
-                row_n[pl.ds(k, 1), :] = a[rows - 1 : rows, :]
-                row_n[pl.ds(k + levels, 1), :] = b[rows - 1 : rows, :]
-                row_s[pl.ds(k, 1), :] = a[0:1, :]
-                row_s[pl.ds(k + levels, 1), :] = b[0:1, :]
-            return packed
-
-        pack[...] = lax.fori_loop(0, levels // STEP, body, zero)
-
-    packing(heat_v, m0_v, pack_1, row_1n, row_1s)
+    def pack_level(k, a, b, packed, row_n, row_s):
+        packed = jnp.where((lane >> 1) == k, pltpu.roll(a, 2 * k + 1, 1), packed)
+        packed = jnp.where(
+            (lane >> 1) == k + levels, pltpu.roll(b, 2 * k + 2 * levels + 1, 1), packed
+        )
+        row_n[pl.ds(k, 1), :] = a[rows - 1 : rows, :]
+        row_n[pl.ds(k + levels, 1), :] = b[rows - 1 : rows, :]
+        row_s[pl.ds(k, 1), :] = a[0:1, :]
+        row_s[pl.ds(k + levels, 1), :] = b[0:1, :]
+        return packed
+
+    def pack_body(block, packed):
+        for i in range(STEP):
+            k = block * STEP + i
+            packed = pack_level(k, heat_v[k], m0_v[k], packed, row_1n, row_1s)
+        return packed
+
+    pack_1[...] = lax.fori_loop(0, levels // STEP, pack_body, zero)
     start(cols_1)
 
     def wide(mine, ew, d, f):
@@ -375,6 +401,12 @@
             result = result + scalar(a) * v
         return result
 
+    def pressed_wide(x):
+        result = 0.0
+        for w, y in zip(face_land, sides(x)):
+            result = result + (PRESS_COEF / math.sqrt(levels)) * w * (x - y)
+        return result
+
     def pressed(x):
         around = sides(x)
         centre = own(x)
@@ -408,10 +440,16 @@
             jnp.where(row == 0, rr[1, pl.ds(k, 1), :], rolled(v, 1, 0)),
         )
 
+    both = jnp.zeros_like(code_w)
+    for k in range(levels):
+        part = COUPLING**2 * (1.0 - k / levels) ** 2 * (k + 0.5) / levels * 2.0 * EOS_QUAD
+        both = both + jnp.where(code_w > float(k), part, 0.0)
+
     arrive(cols_1)
     w2[12] = mixed(rp_1)
 
     def diffuse_body(block, carry):
+        plain, scaled = carry
         rim = w2[12]
         for i in range(2):
             k = block * 2 + i
@@ -425,19 +463,44 @@
                 w = jnp.where(w2[f] > kf, w2[4 + f], 0.0)
                 h_sum = h_sum + w * (h_around[f] - h)
                 m_sum = m_sum + w * (m_around[f] - m)
-            t1_v[k] = jnp.where(code > kf, h_sum, 0.0)
+            wet = code > kf
+            h_sum = jnp.where(wet, h_sum, 0.0)
+            t1_v[k] = h_sum
             u_v[k] = m_sum
-        return carry
-
-    lax.fori_loop(0, levels // 2, diffuse_body, 0)
+            profile = COUPLING * (1.0 - kf / levels)
+            plain = plain + jnp.where(wet, profile * m_sum, 0.0)
+            scaled = scaled + jnp.where(
+                wet,
+                profile * (kf + 0.5) / levels * (1.0 + 2.0 * EOS_QUAD * h_sum),
+                0.0,
+            )
+        return plain, scaled
+
+    plain, scaled = lax.fori_loop(0, levels // 2, diffuse_body, (zero, zero))
+    mine_c[0] = plain
+    mine_c[1] = scaled
+    start(halo_c)
 
     shared(slots_1, recv_g, 1)
     coef = coefficients(totals(slots_1))
-    surface_next = combined(coef, [own(v) for v in basis_1])
+    surface_w = combined(coef, basis_1)
     back_one = combined([pltpu.roll(c, half, 1) for c in coef], basis_2)
-    back_press = pressed(back_one)
-
-    def reverse_body(block, total):
+    back_press_w = pressed_wide(back_one)
+
+    arrive(halo_c)
+    total_zero = (
+        back_one
+        + wide(mine_c, ew_c, d_c, 0)
+        + back_press_w * (wide(mine_c, ew_c, d_c, 1) + both * surface_w)
+    )
+    basis_3, sums_3 = basis(total_zero)
+    vec_2[...] = gathered(sums_3, list(range(ENTRIES)))
+    share(vec_2, slots_2, 2)
+
+    surface_next = own(surface_w)
+    back_press = own(back_press_w)
+
+    def reverse_body(block, packed):
         for i in range(STEP):
             k = block * STEP + i
             kf = level_of(k)
@@ -445,26 +508,19 @@
             second = t1_v[k] + jnp.where(
                 wet, COUPLING * (1.0 - kf / levels) * surface_next, 0.0
             )
-            t1_v[k] = second
             masked = jnp.where(
                 wet,
                 u_v[k]
                 + (kf + 0.5) / levels * (1.0 + 2.0 * EOS_QUAD * second) * back_press,
                 0.0,
             )
+            t1_v[k] = second
             m1_v[k] = masked
-            total = total + COUPLING * (1.0 - kf / levels) * masked
-        return total
-
-    mine_c[0] = lax.fori_loop(0, levels // STEP, reverse_body, own(back_one))
-    start(halo_c)
-    packing(t1_v, m1_v, pack_2, row_2n, row_2s)
+            packed = pack_level(k, second, masked, packed, row_2n, row_2s)
+        return packed
+
+    pack_2[...] = lax.fori_loop(0, levels // STEP, reverse_body, zero)
     start(cols_2)
-
-    arrive(halo_c)
-    basis_3, sums_3 = basis(wide(mine_c, ew_c, d_c, 0))
-    vec_2[...] = gathered(sums_3, list(range(ENTRIES)))
-    share(vec_2, slots_2, 2)
 
     arrive(cols_2)
     w2[13] = mixed(rp_2)
@@ -520,6 +576,7 @@
     levels, rows, lanes = heat.shape
     f32 = jnp.float32
     cube = pltpu.VMEM((levels, rows, lanes), f32)
+    plane = pltpu.VMEM((rows, lanes), f32)
 
     def halos(fields):
         return [
@@ -537,7 +594,7 @@
     ]
     sums = [pltpu.VMEM((1, lanes), f32), pltpu.VMEM((group, 1, lanes), f32)]
     vmem = pl.BlockSpec(memory_space=pltpu.VMEM)
-    hbm = pl.BlockSpec(memory_space=pl.ANY)
+    hbm = pl.BlockSpec(memory_space=pltpu.HBM)
     return pl.pallas_call(
         kernel,
         out_shape=(
@@ -545,18 +602,20 @@
             jax.ShapeDtypeStruct(height.shape, f32),
             jax.ShapeDtypeStruct(height.shape, f32),
         ),
-        in_specs=[hbm, vmem, hbm, vmem, vmem, vmem, vmem],
+        in_specs=[hbm] * 7,
         out_specs=(vmem, vmem, vmem),
-        scratch_shapes=[cube] * 6
+        scratch_shapes=[plane] * 3
+        + [pltpu.VMEM((rows, lanes), jnp.int32)] * 2
+        + [cube] * 6
         + [pltpu.VMEM((14, rows, lanes), f32)]
         + halos(3)
         + halos(2)
-        + halos(1)
+        + halos(2)
         + columns
         + columns
         + sums * 3
         + [
-            pltpu.SemaphoreType.DMA((2,)),
+            pltpu.SemaphoreType.DMA((5 + 2 * CHUNKS,)),
             pltpu.SemaphoreType.DMA((24,)),
             pltpu.SemaphoreType.DMA((24,)),
             pltpu.SemaphoreType.DMA((8,)),
@@ -565,7 +624,7 @@
             pltpu.SemaphoreType.DMA((3,)),
         ],
         compiler_params=pltpu.CompilerParams(
-            collective_id=0, has_side_effects=True, vmem_limit_bytes=40 * 1024 * 1024
+            collective_id=0, has_side_effects=True, vmem_limit_bytes=58 * 1024 * 1024
         ),
     )(*args)
 

time: 33.6 us -> 32.5 us (0.967); the launches traced: 33 us -> 32.2 us
  local copies, waits for them, and re-layouts: 7.67 us -> 3.21 us
  Pallas kernels: 24.6 us -> 28.3 us
    unnamed x17 -> x7, local copies, waits for them, and re-layouts: 7.67 us -> 3.21 us
    pallas_call x1, Pallas kernels: 24.6 us -> 28.3 us  [shards(): pl.pallas_call(kernel, out_shape=(jax.ShapeDtypeStruct(heat.shape, f32),...]
where the time goes in v2:
time: 32.5 us; the launch traced here: 32.2 us
  Pallas kernels  28.3 us (87%)
  local copies, waits for them, and re-layouts  3.21 us (10%)
  between operations  0.65 us (2%)
    pallas_call x1, Pallas kernels, shards(): pl.pallas_call(kernel, out_shape=(jax.ShapeDtypeStruct(heat.shape, f32),...  28.3 us
    unnamed x7, local copies, waits for them, and re-layouts  3.21 us

profile of v2, /device:TPU:0, one launch (start us, length us, event | category | flops | bytes accessed | tf_op | source)
XLA Modules:
  0.0 32.2 jit_solution(5142799779297668326)
XLA Ops:
  0.6 28.3 %shard_map.94 = (f32[32,32,128]{2,1,0:T(8,128)}, f32[32,128]{1,0:T(8,128)}, f32[32,128]{1,0:T(8,128)}) custom-call(f32[32,32,128]{2,1,0:T(8,128)} %heat_hbm.1, f32[32,128]{1,0:T(8,128)} %height_hbm.1, f32[32,32,128]{2,1,0:T(8,128)} %closing_hbm.1, f32[32,128]{1,0:T(8,128)} %closing_height_hbm.1, f32[32,128]{1,0:T(8,128)} %mixing_hbm.1, s32[32,128]{1,0:T(8,128)} %sea_hbm.1, ...), custom_call_target="tpu_custom_call" | custom-call | tf_op jit(solution)/shard_map/pallas_call | solution.py:598
  29.0 0.0 copy-start.1
  29.0 1.9 %copy.13 = f32[32,32,128]{2,1,0:T(8,128)} copy(f32[32,32,128]{2,1,0:T(8,128)} %get-tuple-element.6) | data formatting | bytes 1048576
  30.9 0.0 copy-done.1
  30.9 0.0 copy-start
  30.9 0.6 %copy.14 = f32[32,128]{1,0:T(8,128)} copy(f32[32,128]{1,0:T(8,128)S(1)} %copy-done.1) | data formatting | bytes 32768
  31.5 0.1 copy-done
  31.6 0.6 %copy.15 = f32[32,128]{1,0:T(8,128)} copy(f32[32,128]{1,0:T(8,128)S(1)} %copy-done) | data formatting | bytes 32768
Async XLA Ops:
  29.0 1.9 %copy-start.1 = (f32[32,128]{1,0:T(8,128)S(1)}, f32[32,128]{1,0:T(8,128)}, u32[]{:S(2)}) copy-start(f32[32,128]{1,0:T(8,128)} %get-tuple-element.7) | copy-start | bytes 49156
  30.9 0.7 %copy-start = (f32[32,128]{1,0:T(8,128)S(1)}, f32[32,128]{1,0:T(8,128)}, u32[]{:S(2)}) copy-start(f32[32,128]{1,0:T(8,128)} %get-tuple-element.8) | copy-start | bytes 49156

commit v3 on v2

--- a/solution.py
+++ b/solution.py
@@ -14,9 +14,9 @@
 COUPLING = 1.0
 
 MESH = pl.DeviceIdType.MESH
-RIM = 16
+RIM = 8
 CHUNKS = 4
-STEP = 4
+STEP = 8
 SHIFT = 1.2
 LINK = 0.2
 ENTRIES = 11
@@ -415,6 +415,11 @@
             result = result + w2[8 + i] * (centre - own(around[i]))
         return result * (1.0 / math.sqrt(levels))
 
+    both = jnp.zeros_like(code_w)
+    for k in range(levels):
+        part = COUPLING**2 * (1.0 - k / levels) ** 2 * (k + 0.5) / levels * 2.0 * EOS_QUAD
+        both = both + jnp.where(code_w > float(k), part, 0.0)
+
     arrive(halo_b)
     press_w = wide(mine_b, ew_b, d_b, 0)
     rhs = height_w
@@ -440,19 +445,14 @@
             jnp.where(row == 0, rr[1, pl.ds(k, 1), :], rolled(v, 1, 0)),
         )
 
-    both = jnp.zeros_like(code_w)
-    for k in range(levels):
-        part = COUPLING**2 * (1.0 - k / levels) ** 2 * (k + 0.5) / levels * 2.0 * EOS_QUAD
-        both = both + jnp.where(code_w > float(k), part, 0.0)
-
     arrive(cols_1)
     w2[12] = mixed(rp_1)
 
     def diffuse_body(block, carry):
         plain, scaled = carry
         rim = w2[12]
-        for i in range(2):
-            k = block * 2 + i
+        for i in range(STEP):
+            k = block * STEP + i
             kf = level_of(k)
             h = heat_v[k]
             m = m0_v[k]
@@ -476,7 +476,7 @@
             )
         return plain, scaled
 
-    plain, scaled = lax.fori_loop(0, levels // 2, diffuse_body, (zero, zero))
+    plain, scaled = lax.fori_loop(0, levels // STEP, diffuse_body, (zero, zero))
     mine_c[0] = plain
     mine_c[1] = scaled
     start(halo_c)
@@ -486,6 +486,31 @@
     surface_w = combined(coef, basis_1)
     back_one = combined([pltpu.roll(c, half, 1) for c in coef], basis_2)
     back_press_w = pressed_wide(back_one)
+
+    surface_next = own(surface_w)
+    back_press = own(back_press_w)
+
+    def reverse_body(block, packed):
+        for i in range(STEP):
+            k = block * STEP + i
+            kf = level_of(k)
+            wet = code > kf
+            second = t1_v[k] + jnp.where(
+                wet, COUPLING * (1.0 - kf / levels) * surface_next, 0.0
+            )
+            masked = jnp.where(
+                wet,
+                u_v[k]
+                + (kf + 0.5) / levels * (1.0 + 2.0 * EOS_QUAD * second) * back_press,
+                0.0,
+            )
+            t1_v[k] = second
+            m1_v[k] = masked
+            packed = pack_level(k, second, masked, packed, row_2n, row_2s)
+        return packed
+
+    pack_2[...] = lax.fori_loop(0, levels // STEP, reverse_body, zero)
+    start(cols_2)
 
     arrive(halo_c)
     total_zero = (
@@ -497,35 +522,10 @@
     vec_2[...] = gathered(sums_3, list(range(ENTRIES)))
     share(vec_2, slots_2, 2)
 
-    surface_next = own(surface_w)
-    back_press = own(back_press_w)
-
-    def reverse_body(block, packed):
-        for i in range(STEP):
-            k = block * STEP + i
-            kf = level_of(k)
-            wet = code > kf
-            second = t1_v[k] + jnp.where(
-                wet, COUPLING * (1.0 - kf / levels) * surface_next, 0.0
-            )
-            masked = jnp.where(
-                wet,
-                u_v[k]
-                + (kf + 0.5) / levels * (1.0 + 2.0 * EOS_QUAD * second) * back_press,
-                0.0,
-            )
-            t1_v[k] = second
-            m1_v[k] = masked
-            packed = pack_level(k, second, masked, packed, row_2n, row_2s)
-        return packed
-
-    pack_2[...] = lax.fori_loop(0, levels // STEP, reverse_body, zero)
-    start(cols_2)
-
     arrive(cols_2)
     w2[13] = mixed(rp_2)
 
-    def gradient_body(k, total):
+    def gradient_level(k, total):
         kf = level_of(k)
         h, m0, t, m1 = heat_v[k], m0_v[k], t1_v[k], m1_v[k]
         shift = 127 - 2 * k
@@ -545,7 +545,12 @@
         u_v[k] = spread
         return total
 
-    diff_ref[...] = -0.5 * lax.fori_loop(0, levels, gradient_body, zero)
+    def gradient_body(block, total):
+        for i in range(STEP):
+            total = gradient_level(block * STEP + i, total)
+        return total
+
+    diff_ref[...] = -0.5 * lax.fori_loop(0, levels // STEP, gradient_body, zero)
 
     shared(slots_2, recv_g, 2)
     surface = combined(coefficients(totals(slots_2)), basis_3)

time: 32.5 us -> 27.3 us (0.84)
  Pallas kernels: 28.3 us -> 23.1 us
    pallas_call x1, Pallas kernels: 28.3 us -> 23.1 us  [shards(): pl.pallas_call(kernel, out_shape=(jax.ShapeDtypeStruct(heat.shape, f32),...]
where the time goes in v3:
time: 27.3 us; the launch traced here: 27 us
  Pallas kernels  23.1 us (85%)
  local copies, waits for them, and re-layouts  3.21 us (12%)
  between operations  0.65 us (2%)
    pallas_call x1, Pallas kernels, shards(): pl.pallas_call(kernel, out_shape=(jax.ShapeDtypeStruct(heat.shape, f32),...  23.1 us
    unnamed x7, local copies, waits for them, and re-layouts  3.21 us

profile of v3, /device:TPU:0, one launch (start us, length us, event | category | flops | bytes accessed | tf_op | source)
XLA Modules:
  0.0 27.0 jit_solution(823439515854194894)
XLA Ops:
  0.6 23.1 %shard_map.94 = (f32[32,32,128]{2,1,0:T(8,128)}, f32[32,128]{1,0:T(8,128)}, f32[32,128]{1,0:T(8,128)}) custom-call(f32[32,32,128]{2,1,0:T(8,128)} %heat_hbm.1, f32[32,128]{1,0:T(8,128)} %height_hbm.1, f32[32,32,128]{2,1,0:T(8,128)} %closing_hbm.1, f32[32,128]{1,0:T(8,128)} %closing_height_hbm.1, f32[32,128]{1,0:T(8,128)} %mixing_hbm.1, s32[32,128]{1,0:T(8,128)} %sea_hbm.1, ...), custom_call_target="tpu_custom_call" | custom-call | tf_op jit(solution)/shard_map/pallas_call | solution.py:603
  23.7 0.0 copy-start.1
  23.7 1.9 %copy.13 = f32[32,32,128]{2,1,0:T(8,128)} copy(f32[32,32,128]{2,1,0:T(8,128)} %get-tuple-element.6) | data formatting | bytes 1048576
  25.6 0.0 copy-done.1
  25.6 0.0 copy-start
  25.6 0.6 %copy.14 = f32[32,128]{1,0:T(8,128)} copy(f32[32,128]{1,0:T(8,128)S(1)} %copy-done.1) | data formatting | bytes 32768
  26.2 0.1 copy-done
  26.4 0.6 %copy.15 = f32[32,128]{1,0:T(8,128)} copy(f32[32,128]{1,0:T(8,128)S(1)} %copy-done) | data formatting | bytes 32768
Async XLA Ops:
  23.7 1.9 %copy-start.1 = (f32[32,128]{1,0:T(8,128)S(1)}, f32[32,128]{1,0:T(8,128)}, u32[]{:S(2)}) copy-start(f32[32,128]{1,0:T(8,128)} %get-tuple-element.7) | copy-start | bytes 49156
  25.6 0.7 %copy-start = (f32[32,128]{1,0:T(8,128)S(1)}, f32[32,128]{1,0:T(8,128)}, u32[]{:S(2)}) copy-start(f32[32,128]{1,0:T(8,128)} %get-tuple-element.8) | copy-start | bytes 49156
